TPU v7x, 512 devices: a whole 4x4x16 slice. The times are simulated.
512 devices in a mesh: tm: 64 (over x, z), mp: 8 (over y, core).
Axes of the slice: x: 4, y: 4, z: 16, core: 2. Of those that a mesh axis runs over, the one named last changes fastest.
Arguments:
- observations: bfloat16 [64, 4096, 256], P('tm', None, 'mp'), may hold values from -6 to 6
- contact: int32 [512, 8, 8], P('tm'), may hold values 0 or 1
- resets: int32 [8, 4096], P(None, 'tm'), may hold values 0 or 1
- q_weight: bfloat16 [2048, 1024], P(None, 'mp'), may hold values from -0.125 to 0.125
- k_weight: bfloat16 [2048, 1024], P(None, 'mp'), may hold values from -0.125 to 0.125
- v_weight: bfloat16 [2048, 1024], P(None, 'mp'), may hold values from -0.125 to 0.125
- decay_weight: bfloat16 [2048, 1024], P(None, 'mp'), may hold values from -0.125 to 0.125
- gate_weight: bfloat16 [2048, 1024], P(None, 'mp'), may hold values from -0.125 to 0.125
- decay_bias: float32 [8, 128], P('mp'), may hold values from 4 to 14
- norm_gain: float32 [8, 128], P('mp'), may hold values from 0.25 to 1.75
- out_weight: bfloat16 [1024, 2048], P(None, 'mp'), may hold values from -0.1875 to 0.1875
- out_cotangent: bfloat16 [8, 4096, 2048], P(None, 'tm', 'mp'), may hold values from -0.03125 to 0.03125
Outputs:
- following_frame: bfloat16 [8, 4096, 2048], P(None, 'tm', 'mp')
- out_weight_grad: float32 [1024, 2048], P('tm', 'mp')
All inputs are finite; a program needn't handle non-finite values. No bound on the sum of `contact` or of `resets` on one device may be relied on, other than what follows from the above.
Results may differ from a plain program's by a relative error of at most 0.0049.
Values may be sent and summed in bfloat16 or wider, within the bound.
A program may use at most 128 MiB of HBM per device.

v0:
```python
import jax
import jax.numpy as jnp
from jax import lax
from jax.sharding import PartitionSpec as P

HK = 128
CH = 8


def prefix(part, axis, combine, identity):
    place = lax.axis_index(axis)
    gathered = jax.tree.map(lambda a: lax.all_gather(a, axis), part)
    state = jax.tree.map(lambda a, e: jnp.zeros_like(a) + jnp.asarray(e, a.dtype), part, identity)

    def one(hop, state):
        return combine(
            state, jax.tree.map(lambda a: lax.dynamic_index_in_dim(a, hop, 0, False), gathered)
        )

    return lax.fori_loop(0, place, one, state)


def block_terms(queries, key_rows, value_rows, log_decay, reset_block):
    frames = queries.shape[2]
    log_total = jnp.cumsum(log_decay, axis=2)
    resets_observed = jnp.cumsum(reset_block, axis=1)
    last_total = log_total[:, :, -1, :]
    last_seen = resets_observed[:, -1]
    untouched = (resets_observed == 0).astype(jnp.float32)[:, None, :, None]
    survives = (resets_observed == last_seen[:, None]).astype(jnp.float32)[:, None, :, None]
    block_decay = jnp.exp(last_total) * (last_seen == 0).astype(jnp.float32)[:, None, None]
    weights = jnp.exp(last_total[:, :, None, :] - log_total) * survives
    block_state = jnp.einsum(
        "chtk,chtv->chkv", key_rows * weights, value_rows, precision=lax.Precision.HIGHEST
    )
    carried_q = queries * jnp.exp(log_total) * untouched
    middle = log_total[:, :, frames // 2 : frames // 2 + 1, :]
    scaled_q = queries * jnp.exp(log_total - middle)
    scaled_k = key_rows * jnp.exp(middle - log_total)
    scores = jnp.einsum("chtk,chsk->chts", scaled_q, scaled_k, precision=lax.Precision.HIGHEST)
    row_index = lax.broadcasted_iota(jnp.int32, (frames, frames), 0)
    earlier = lax.broadcasted_iota(jnp.int32, (frames, frames), 1)
    causal = (row_index >= earlier)[None, :, :] & (
        resets_observed[:, :, None] == resets_observed[:, None, :]
    )
    scores = jnp.where(causal[:, None, :, :], scores, 0.0)
    inside = jnp.einsum("chts,chsv->chtv", scores, value_rows, precision=lax.Precision.HIGHEST)
    return (block_decay, block_state, carried_q, inside)


def finish(attended, gate_values, gain_head, links_block):
    characters, head_count, frames, value_width = attended.shape
    blocks = links_block.shape[0]
    mean_square = jnp.mean(attended * attended, axis=-1, keepdims=True)
    normed = attended * lax.rsqrt(mean_square + 1e-06) * gain_head[None, :, None, :]
    normed = normed.transpose(0, 2, 1, 3).reshape(characters, frames, head_count * value_width)
    regrouped_rows = normed.reshape(characters, blocks, frames // blocks * head_count * value_width)
    contact_factor = links_block.astype(jnp.float32)
    total_rows = jnp.einsum(
        "nmr,rnd->mnd", contact_factor, regrouped_rows, precision=lax.Precision.HIGHEST
    )
    partners = jnp.maximum(jnp.sum(contact_factor, axis=-1), 1.0)
    mixed_rows = regrouped_rows + total_rows / jnp.transpose(partners)[:, :, None]
    mixed_rows = mixed_rows.reshape(characters, frames, head_count * value_width)
    return (mixed_rows * jax.nn.silu(gate_values)).astype(jnp.bfloat16)


def combine_states(earlier, later_part):
    return (earlier[0] * later_part[0], later_part[0][..., None] * earlier[1] + later_part[1])


def local(
    observations,
    contact,
    resets,
    q_weight,
    k_weight,
    v_weight,
    decay_weight,
    gate_weight,
    decay_bias,
    norm_gain,
    out_weight,
    out_cotangent,
):
    span_time = lax.axis_size("tm")
    splits = span_time // CH
    characters = resets.shape[0]
    frames = resets.shape[1]
    head_count = decay_bias.shape[0]
    matrices = (q_weight, k_weight, v_weight, decay_weight, gate_weight)
    zero_sums = tuple(
        (jnp.zeros((characters, frames, matrix.shape[1]), jnp.float32) for matrix in matrices)
    )
    full_rows = lax.all_gather(observations, "mp", axis=2, tiled=True)
    rollout = lax.all_to_all(full_rows, "tm", split_axis=1, concat_axis=0, tiled=True)
    span_width = rollout.shape[2]
    regrouped_rows = rollout.reshape(characters, splits, frames, span_width)
    result = []
    for partial_sum, matrix in zip(zero_sums, matrices):
        blocked = matrix.reshape(splits, matrix.shape[0] // splits, matrix.shape[1])
        result.append(
            jnp.einsum("cgtf,gfh->cth", regrouped_rows, blocked, preferred_element_type=jnp.float32)
        )
    projected = tuple(result)

    def head_major(values):
        return values.reshape(characters, frames, head_count, -1).transpose(0, 2, 1, 3)

    queries = head_major(projected[0] * HK ** (-0.5))
    key_rows = head_major(projected[1])
    value_rows = head_major(projected[2])
    log_decay = head_major(
        jax.nn.log_sigmoid(projected[3].reshape(characters, frames, head_count, -1) + decay_bias)
    )
    block_decay, block_state, carried_q, inside = block_terms(
        queries, key_rows, value_rows, log_decay, resets
    )
    identity = (jnp.ones_like(block_decay), jnp.zeros_like(block_state))
    entering = prefix((block_decay, block_state), "tm", combine_states, identity)
    attended = inside + jnp.einsum(
        "chtk,chkv->chtv", carried_q, entering[1], precision=lax.Precision.HIGHEST
    )
    gated = finish(attended, projected[4], norm_gain, contact)
    gated_rows = gated.reshape(characters * frames, -1)
    cotangent_rows = out_cotangent.reshape(characters * frames, -1)
    portion = lax.all_gather(gated_rows, "mp", axis=1, tiled=True)
    produced = jnp.dot(portion, out_weight, preferred_element_type=jnp.float32)
    gradient_piece = lax.dot_general(
        portion, cotangent_rows, (((0,), (0,)), ((), ())), preferred_element_type=jnp.float32
    )
    produced, partial_grad = (produced, gradient_piece)
    following_frame = produced.astype(jnp.bfloat16).reshape(characters, frames, -1)
    weight_grad = lax.psum_scatter(partial_grad, "tm", scatter_dimension=0, tiled=True)
    return (following_frame, weight_grad)


def solution(mesh):
    placed = (
        P("tm", None, "mp"),
        P("tm", None, None),
        P(None, "tm"),
        P(None, "mp"),
        P(None, "mp"),
        P(None, "mp"),
        P(None, "mp"),
        P(None, "mp"),
        P("mp", None),
        P("mp", None),
        P(None, "mp"),
        P(None, "tm", "mp"),
    )
    return jax.shard_map(
        local,
        mesh=mesh,
        in_specs=placed,
        out_specs=(P(None, "tm", "mp"), P("tm", "mp")),
        check_vma=False,
    )
```

profile of v0, /device:TPU:8, one launch (start us, length us, event | category | flops | bytes accessed | tf_op | source)
XLA Modules:
  0.0 1353.7 jit_solution(6704598011931905069)
XLA Ops:
  7.2 0.7 all-gather.5.cloned.1.call-update
  7.9 38.6 %all-gather.5.cloned.1.call-done = bf16[1,4096,256]{1,2,0:T(8,128)(2,1)} async-done(((bf16[1,4096,32]{1,2,0:T(8,128)(2,1)}), bf16[1,4096,256]{1,2,0:T(8,128)(2,1)}) %all-gather.5.cloned.1.call-update) | async-done | bytes 2097168 | tf_op jit(solution)/shard_map/all_gather | solution.py:95
  46.5 10.0 copy.41
  57.0 21.6 %reduce.4 = bf16[4096,256]{1,0:T(8,128)(2,1)S(1)} reduce(bf16[4096,1,256]{2,1,0:T(2,128)(2,1)} %bitcast.127, bf16[]{:T(256)} %broadcast.79), dimensions={1}, to_apply=%bitcast.99.reduce_sub_computation | reduce | bytes 4194306
  78.6 2.1 reshape.229
  80.7 15.7 %all-to-all-start = ((bf16[64,2,8192]{2,1,0:T(2,128)(2,1)}), bf16[64,2,8192]{2,1,0:T(2,128)(2,1)S(1)}, u32[]{:S(2)}, u32[]{:S(2)}) async-start(bf16[64,2,8192]{2,1,0:T(2,128)(2,1)} %reshape.229), calls=%async_computation | async-start | bytes 4194304 | tf_op jit(solution)/shard_map/all_to_all | solution.py:96
  97.0 97.4 %all-to-all-done = bf16[64,2,8192]{2,1,0:T(2,128)(2,1)S(1)} async-done(((bf16[64,2,8192]{2,1,0:T(2,128)(2,1)}), bf16[64,2,8192]{2,1,0:T(2,128)(2,1)S(1)}, u32[]{:S(2)}, u32[]{:S(2)}) %all-to-all-start) | async-done | bytes 2097184 | tf_op jit(solution)/shard_map/all_to_all | solution.py:96
  194.4 6.7 reshape.230
  201.1 2.5 copy.53
  203.7 0.7 convolution_bitcast_fusion.2
  204.7 0.8 fusion.7
  205.7 0.7 convolution_bitcast_fusion.1
  206.4 1.9 fusion.20
  208.6 87.3 %all_gather.17 = f32[64,8,1,128]{3,1,2,0:T(8,128)} all-gather(f32[1,8,1,128]{3,1,2,0:T(8,128)S(1)} %bitcast_multiply_fusion), channel_id=1, replica_groups=mesh['tm'=64,'mp'=8] {'tm'}, dimensions={0}, use_global_device_ids=true | all-gather | bytes 266240 | tf_op jit(solution)/shard_map/all_gather | solution.py:12
  295.9 1.9 fusion
  297.9 0.7 copy-done.1
  299.2 1.1 fusion.33
  300.3 196.3 %all-gather.9.cloned.1.call-done = f32[512,128,128]{2,1,0:T(8,128)} async-done(((f32[8,128,128]{2,1,0:T(8,128)}), f32[512,128,128]{2,1,0:T(8,128)}) %all-gather.9.cloned.1.call-update) | async-done | bytes 33554448 | tf_op jit(solution)/shard_map/all_gather | solution.py:12
  496.8 1.8 multiply_reduce_fusion
  499.6 2.5 multiply_convert_fusion
  502.1 147.1 %all-gather.7.cloned.1.call-done = bf16[512,1024]{1,0:T(8,128)(2,1)} async-done(((bf16[512,128]{1,0:T(8,128)(2,1)}), bf16[512,1024]{1,0:T(8,128)(2,1)}) %all-gather.7.cloned.1.call-update) | async-done | bytes 1048592 | tf_op jit(solution)/shard_map/all_gather | solution.py:127
  649.2 2.8 fusion.34
  652.1 1.1 convolution_convert_fusion
  653.2 693.9 %reduce-scatter.2.cloned.1.call-done = f32[16,256]{1,0:T(8,128)} async-done(((f32[1024,256]{1,0:T(8,128)}), f32[16,256]{1,0:T(8,128)}) %reduce-scatter.2.cloned.1.call-update) | async-done | bytes 16400 | tf_op jit(solution)/shard_map/reduce_scatter | solution.py:134
  (48 shorter events, 3.8 us)
Async XLA Ops:
  7.2 196.5 %copy-start = (bf16[2048,128]{1,0:T(8,128)(2,1)S(1)}, bf16[2048,128]{1,0:T(8,128)(2,1)}, u32[]{:S(2)}) copy-start(bf16[2048,128]{1,0:T(8,128)(2,1)} %param.18) | copy-start | bytes 1572868
  7.2 39.3 %all-gather.5.cloned.1.call-start = ((), (), s32[]{:S(2)}) async-start(), calls=%async_computation.2 | async-start | bytes 2359296 | tf_op jit(solution)/shard_map/all_gather | solution.py:95
  80.7 15.8 %copy-start.5 = (s32[8,64]{1,0:T(8,128)S(1)}, s32[8,64]{1,0:T(8,128)}, u32[]{:S(2)}) copy-start(s32[8,64]{1,0:T(8,128)} %param.16) | copy-start | bytes 6148
  80.7 113.6 %all-to-all-start = ((bf16[64,2,8192]{2,1,0:T(2,128)(2,1)}), bf16[64,2,8192]{2,1,0:T(2,128)(2,1)S(1)}, u32[]{:S(2)}, u32[]{:S(2)}) async-start(bf16[64,2,8192]{2,1,0:T(2,128)(2,1)} %reshape.229), calls=%async_computation | async-start | bytes 4194304 | tf_op jit(solution)/shard_map/all_to_all | solution.py:96
  96.5 400.1 %all-gather.9.cloned.1.call-start = ((), (), s32[]{:S(2)}) async-start(), calls=%async_computation.5 | async-start | bytes 34078720 | tf_op jit(solution)/shard_map/all_gather | solution.py:12
  203.6 1.0 copy-start.7
  203.7 1.0 copy-start.10
  204.7 1.0 copy-start.8
  205.7 2.7 copy-start.4
  208.4 440.8 %all-gather.7.cloned.1.call-start = ((), (), s32[]{:S(2)}) async-start(), calls=%async_computation.3 | async-start | bytes 1179648 | tf_op jit(solution)/shard_map/all_gather | solution.py:127
  297.8 0.7 copy-start.1
  496.6 2.0 copy-start.6
  499.6 149.7 %copy-start.3 = (bf16[8,64,256]{2,1,0:T(8,128)(2,1)S(1)}, bf16[8,64,256]{2,1,0:T(8,128)(2,1)}, u32[]{:S(2)}) copy-start(bf16[8,64,256]{2,1,0:T(8,128)(2,1)} %param.25) | copy-start | bytes 786436
  502.1 150.0 %copy-start.9 = (bf16[1024,256]{1,0:T(8,128)(2,1)S(1)}, bf16[1024,256]{1,0:T(8,128)(2,1)}, u32[]{:S(2)}) copy-start(bf16[1024,256]{1,0:T(8,128)(2,1)} %param.24) | copy-start | bytes 1572868
  502.1 845.1 %reduce-scatter.2.cloned.1.call-start = ((), (), s32[]{:S(2)}) async-start(), calls=%async_computation.4 | async-start | bytes 1064960 | tf_op jit(solution)/shard_map/reduce_scatter | solution.py:134
  649.2 2.9 copy-start.2
Sparse Core Ops, SparseCore 0:
  10.2 36.2 all-gather.4
  208.5 287.9 all-gather.8
  502.2 146.9 all-gather.6
  654.0 693.0 reduce-scatter.1
where the time goes:
time: 1360 us; the launch traced here: 1350 us
  waiting for transfers between devices  1170 us (86%)
  blocking collectives  87.3 us (6%)
  local copies, waits for them, and re-layouts  23.5 us (2%)
  other arithmetic  22.3 us (2%)
  matrix products  16.5 us (1%)
  starting transfers between devices  15.9 us (1%)
  between operations  14 us (1%)
    reduce_scatter x1, waiting for transfers between devices, local(): lax.psum_scatter(partial_grad, 'tm', scatter_dimension=0, tiled=True)  694 us
    all_gather x1, waiting for transfers between devices, prefix(): gathered = jax.tree.map(lambda a: lax.all_gather(a, axis), part)  196 us
    all_gather x1, waiting for transfers between devices, local(): portion = lax.all_gather(gated_rows, 'mp', axis=1, tiled=True)  147 us
    all_to_all x1, waiting for transfers between devices, local(): lax.all_to_all(full_rows, 'tm', split_axis=1, concat_axis=0, tiled=True)  97.4 us
    all_gather x1, blocking collectives, prefix(): gathered = jax.tree.map(lambda a: lax.all_gather(a, axis), part)  87.3 us
    all_gather x1, waiting for transfers between devices, local(): full_rows = lax.all_gather(observations, 'mp', axis=2, tiled=True)  38.6 us
  transfers between devices with their start and end apart: 5, of which 5 were waited for; matrix products, arithmetic and copies ran while one was open for 0% of the time, Pallas kernels for 0%

commit v1 on v0

--- a/solution.py
+++ b/solution.py
@@ -124,7 +124,12 @@
     gated = finish(attended, projected[4], norm_gain, contact)
     gated_rows = gated.reshape(characters * frames, -1)
     cotangent_rows = out_cotangent.reshape(characters * frames, -1)
-    portion = lax.all_gather(gated_rows, "mp", axis=1, tiled=True)
+    ring = [gated_rows]
+    for hop_ in range(7):
+        ring.append(lax.ppermute(ring[-1], "mp", [(dev, (dev + 1) % 8) for dev in range(8)]))
+    portion = jnp.roll(
+        jnp.concatenate(ring[::-1], axis=1), (lax.axis_index("mp") + 1) * ring[0].shape[1], axis=1
+    )
     produced = jnp.dot(portion, out_weight, preferred_element_type=jnp.float32)
     gradient_piece = lax.dot_general(
         portion, cotangent_rows, (((0,), (0,)), ((), ())), preferred_element_type=jnp.float32

time: 1360 us -> 1360 us (level)
    all_gather x1 -> x0, waiting for transfers between devices: 147 us -> none  [local(): portion = lax.all_gather(gated_rows, 'mp', axis=1, tiled=True)]
    reduce_scatter x1, waiting for transfers between devices: 694 us -> 812 us  [local(): lax.psum_scatter(partial_grad, 'tm', scatter_dimension=0, tiled=True)]
    ppermute x0 -> x7, waiting for transfers between devices: none -> 32.2 us  [local(): lax.ppermute(ring[-1], 'mp', [(dev, (dev + 1) % 8) for dev in range(8)])]
  transfers between devices with their start and end apart: 5 -> 11, of which waited for: 5 -> 11; matrix products, arithmetic and copies ran while one was open for 0% -> 0% of each run, Pallas kernels for 0% -> 0%
where the time goes in v1:
time: 1360 us
  waiting for transfers between devices  1180 us (87%)
  blocking collectives  87 us (6%)
  local copies, waits for them, and re-layouts  25.9 us (2%)
  other arithmetic  22.3 us (2%)
  starting transfers between devices  15.9 us (1%)
  matrix products  14.5 us (1%)
  between operations  14.1 us (1%)
    reduce_scatter x1, waiting for transfers between devices, local(): lax.psum_scatter(partial_grad, 'tm', scatter_dimension=0, tiled=True)  812 us
    all_gather x1, waiting for transfers between devices, prefix(): gathered = jax.tree.map(lambda a: lax.all_gather(a, axis), part)  197 us
    all_to_all x1, waiting for transfers between devices, local(): lax.all_to_all(full_rows, 'tm', split_axis=1, concat_axis=0, tiled=True)  97.4 us
    all_gather x1, blocking collectives, prefix(): gathered = jax.tree.map(lambda a: lax.all_gather(a, axis), part)  87 us
    all_gather x1, waiting for transfers between devices, local(): full_rows = lax.all_gather(observations, 'mp', axis=2, tiled=True)  38.6 us
    ppermute x7, waiting for transfers between devices, local(): lax.ppermute(ring[-1], 'mp', [(dev, (dev + 1) % 8) for dev in range(8)])  32.2 us
  transfers between devices with their start and end apart: 11, of which 11 were waited for; matrix products, arithmetic and copies ran while one was open for 0% of the time, Pallas kernels for 0%

profile of v1, /device:TPU:8, one launch (start us, length us, event | category | flops | bytes accessed | tf_op | source)
XLA Modules:
  0.0 1357.8 jit_solution(1351628585651975578)
XLA Ops:
  7.9 38.6 %all-gather.4.cloned.1.call-done = bf16[1,4096,256]{1,2,0:T(8,128)(2,1)} async-done(((bf16[1,4096,32]{1,2,0:T(8,128)(2,1)}), bf16[1,4096,256]{1,2,0:T(8,128)(2,1)}) %all-gather.4.cloned.1.call-update) | async-done | bytes 2097168 | tf_op jit(solution)/shard_map/all_gather | solution.py:95
  46.5 10.0 copy.41
  57.0 21.6 %reduce.4 = bf16[4096,256]{1,0:T(8,128)(2,1)S(1)} reduce(bf16[4096,1,256]{2,1,0:T(2,128)(2,1)} %bitcast.125, bf16[]{:T(256)} %broadcast.80), dimensions={1}, to_apply=%bitcast.99.reduce_sub_computation | reduce | bytes 4194306
  78.6 2.0 reshape.229
  80.6 15.7 %all-to-all-start = ((bf16[64,2,8192]{2,1,0:T(2,128)(2,1)}), bf16[64,2,8192]{2,1,0:T(2,128)(2,1)S(1)}, u32[]{:S(2)}, u32[]{:S(2)}) async-start(bf16[64,2,8192]{2,1,0:T(2,128)(2,1)} %reshape.229), calls=%async_computation | async-start | bytes 4194304 | tf_op jit(solution)/shard_map/all_to_all | solution.py:96
  96.9 97.4 %all-to-all-done = bf16[64,2,8192]{2,1,0:T(2,128)(2,1)S(1)} async-done(((bf16[64,2,8192]{2,1,0:T(2,128)(2,1)}), bf16[64,2,8192]{2,1,0:T(2,128)(2,1)S(1)}, u32[]{:S(2)}, u32[]{:S(2)}) %all-to-all-start) | async-done | bytes 2097184 | tf_op jit(solution)/shard_map/all_to_all | solution.py:96
  194.3 6.7 reshape.230
  201.0 2.5 copy.53
  206.4 1.9 fusion.23
  208.6 87.0 %all_gather.14 = f32[64,8,1,128]{3,1,2,0:T(8,128)} all-gather(f32[1,8,1,128]{3,1,2,0:T(8,128)S(1)} %bitcast_multiply_fusion), channel_id=1, replica_groups=mesh['tm'=64,'mp'=8] {'tm'}, dimensions={0}, use_global_device_ids=true | all-gather | bytes 266240 | tf_op jit(solution)/shard_map/all_gather | solution.py:12
  295.6 1.9 fusion
  299.9 196.8 %all-gather.6.cloned.1.call-done = f32[512,128,128]{2,1,0:T(8,128)} async-done(((f32[8,128,128]{2,1,0:T(8,128)}), f32[512,128,128]{2,1,0:T(8,128)}) %all-gather.6.cloned.1.call-update) | async-done | bytes 33554448 | tf_op jit(solution)/shard_map/all_gather | solution.py:12
  496.9 1.8 multiply_reduce_fusion
  499.8 1.8 multiply_convert_fusion
  501.5 4.4 collective-permute-done
  505.9 4.4 collective-permute-done.1
  510.3 4.4 collective-permute-done.2
  514.7 4.4 collective-permute-done.3
  519.1 4.4 collective-permute-done.4
  523.5 4.6 collective-permute-done.5
  528.1 5.7 collective-permute-done.6
  536.4 1.5 fusion.5
  537.9 1.2 convolution_convert_fusion
  539.0 812.2 %reduce-scatter.2.cloned.1.call-done = f32[16,256]{1,0:T(8,128)} async-done(((f32[1024,256]{1,0:T(8,128)}), f32[16,256]{1,0:T(8,128)}) %reduce-scatter.2.cloned.1.call-update) | async-done | bytes 16400 | tf_op jit(solution)/shard_map/reduce_scatter | solution.py:139
  (73 shorter events, 10.8 us)
Async XLA Ops:
  7.2 196.4 %copy-start = (bf16[2048,128]{1,0:T(8,128)(2,1)S(1)}, bf16[2048,128]{1,0:T(8,128)(2,1)}, u32[]{:S(2)}) copy-start(bf16[2048,128]{1,0:T(8,128)(2,1)} %param.18) | copy-start | bytes 1572868
  7.2 39.3 %all-gather.4.cloned.1.call-start = ((), (), s32[]{:S(2)}) async-start(), calls=%async_computation.2 | async-start | bytes 2359296 | tf_op jit(solution)/shard_map/all_gather | solution.py:95
  80.6 15.8 %copy-start.4 = (s32[8,64]{1,0:T(8,128)S(1)}, s32[8,64]{1,0:T(8,128)}, u32[]{:S(2)}) copy-start(s32[8,64]{1,0:T(8,128)} %param.16) | copy-start | bytes 6148
  80.6 113.6 %all-to-all-start = ((bf16[64,2,8192]{2,1,0:T(2,128)(2,1)}), bf16[64,2,8192]{2,1,0:T(2,128)(2,1)S(1)}, u32[]{:S(2)}, u32[]{:S(2)}) async-start(bf16[64,2,8192]{2,1,0:T(2,128)(2,1)} %reshape.229), calls=%async_computation | async-start | bytes 4194304 | tf_op jit(solution)/shard_map/all_to_all | solution.py:96
  96.4 400.3 %all-gather.6.cloned.1.call-start = ((), (), s32[]{:S(2)}) async-start(), calls=%async_computation.4 | async-start | bytes 34078720 | tf_op jit(solution)/shard_map/all_gather | solution.py:12
  203.6 1.0 copy-start.6
  203.6 1.0 copy-start.9
  204.6 1.0 copy-start.7
  205.7 2.7 copy-start.3
  208.3 1142.9 %reduce-scatter.2.cloned.1.call-start = ((), (), s32[]{:S(2)}) async-start(), calls=%async_computation.3 | async-start | bytes 1064960 | tf_op jit(solution)/shard_map/reduce_scatter | solution.py:139
  297.5 0.7 copy-start.1
  496.7 2.0 copy-start.5
  501.5 4.4 collective-permute-start
  505.9 4.4 collective-permute-start.1
  510.3 4.4 collective-permute-start.2
  514.7 4.4 collective-permute-start.3
  519.1 4.4 collective-permute-start.4
  523.5 4.6 collective-permute-start.5
  528.1 5.7 collective-permute-start.6
  528.1 8.3 copy-start.2
  536.2 1.6 copy-start.8
Sparse Core Ops, SparseCore 0:
  10.2 36.2 all-gather.3
  208.5 288.1 all-gather.5
  538.0 813.2 reduce-scatter.1
